TPU v7x, 32 devices: a whole 2x2x4 slice. The times are simulated.
32 devices in a mesh: groups: 2 (over y), tiles: 4 (over z), cols: 2 (over core), dates: 2 (over x).
Axes of the slice: x: 2, y: 2, z: 4, core: 2. Of those that a mesh axis runs over, the one named last changes fastest.
Arguments:
- imagery: bfloat16 [8, 4, 432, 4096], P(('groups', 'tiles'), 'cols', 'dates'), parts along dimension 0, may hold values from -6 to 6
- pixel_mask: int32 [8, 4, 4096], P(('groups', 'tiles'), ('cols', 'dates')), parts along dimension 0, may hold values 0 or 1
- point_pixel: int32 [8, 4, 4096], P(('groups', 'tiles'), ('cols', 'dates')), parts along dimension 0, may hold values from 0 to 4095
- point_yield: float32 [8, 4, 4096], P(('groups', 'tiles'), ('cols', 'dates')), parts along dimension 0, may hold values from -6 to 6
Outputs:
- prediction: float32 [8, 4, 4096], P(('groups', 'tiles'), ('cols', 'dates')), parts along dimension 0
- distance: float32 [8, 4, 4096], P(('groups', 'tiles'), ('cols', 'dates')), parts along dimension 0
- residual: float32 [8, 4, 4096], P(('groups', 'tiles'), ('cols', 'dates')), parts along dimension 0
There are 2 independent parts, one for each index of `groups`. A program takes and returns all parts, laid end to end along the dimension named above; each array names one. Nothing has to cross between parts.
All inputs are finite; a program needn't handle non-finite values. No bound on the sum of `pixel_mask` on one device may be relied on, other than what follows from the above.
Results may differ from a plain program's by a relative error of at most 0.0003.
Values may be sent and summed in bfloat16 or wider, within the bound.
A program may use at most 128 MiB of HBM per device.

v0:
```python
import functools

import jax
import jax.numpy as jnp
from jax import lax
from jax.experimental import pallas as pl
from jax.experimental.pallas import tpu as pltpu
from jax.sharding import PartitionSpec as P

ridge_term = 0.05
LANES = 128
CHUNK = 512
PIECES = 8
F32 = jnp.float32
BF16 = jnp.bfloat16
NT = (((1,), (1,)), ((), ()))


def split3(x):
    a = x.astype(BF16)
    rest = x - a.astype(F32)
    b = rest.astype(BF16)
    c = (rest - b.astype(F32)).astype(BF16)
    return a, b, c


def one_hots(index, rows):
    points = index.shape[1]
    high = lax.broadcasted_iota(jnp.int32, (rows, points), 0) == index // LANES
    low = lax.broadcasted_iota(jnp.int32, (LANES, points), 0) == index % LANES
    return high, low


def segment_kernel(index_ref, yield_ref, mask_ref, weight_ref, product_ref):
    rows = mask_ref.shape[0]
    high, low = one_hots(index_ref[...], rows)
    low = jnp.where(low, 1.0, 0.0).astype(BF16)
    pieces = [jnp.where(high, 1.0, 0.0).astype(BF16)]
    for piece in split3(yield_ref[...]):
        pieces.append(jnp.where(high, piece.astype(F32), 0.0).astype(BF16))
    sums = lax.dot_general(
        jnp.concatenate(pieces, 0), low, NT, preferred_element_type=F32
    )
    counts = sums[:rows]
    totals = sums[rows : 2 * rows] + sums[2 * rows : 3 * rows] + sums[3 * rows :]
    weight = jnp.where(counts > 0, mask_ref[...].astype(F32), 0.0)
    weight_ref[...] = weight
    product_ref[...] = weight * (totals / jnp.maximum(counts, 1.0))


def bands(width):
    blocks, offset = [], 0
    for i in range(pl.cdiv(width, LANES)):
        height = min(LANES, width - i * LANES)
        for j in range(i + 1):
            blocks.append((i, j, height, offset))
            offset += height
    return blocks, offset


def gram_kernel(feats_ref, weight_ref, product_ref, out_ref, acc):
    width, pixels = feats_ref.shape
    acc[...] = jnp.zeros_like(acc)

    def step(c, _):
        at = pl.multiple_of(c * CHUNK, CHUNK)
        feats = feats_ref[:, pl.ds(at, CHUNK)]
        left = []
        for s in range(CHUNK // LANES):
            row = pl.ds(c * (CHUNK // LANES) + s, 1)
            part = feats[:, s * LANES : (s + 1) * LANES]
            scaled = part * weight_ref[row, :].astype(BF16)
            a, b, d = (p.astype(F32) for p in split3(product_ref[row, :]))
            line = lax.broadcasted_iota(jnp.int32, (16, LANES), 0)
            extra = jnp.where(
                line == 0, a, jnp.where(line == 1, b, jnp.where(line == 2, d, 0.0))
            )
            left.append(jnp.concatenate([scaled, extra.astype(BF16)], 0))
        acc[...] += lax.dot_general(
            jnp.concatenate(left, 1), feats, NT, preferred_element_type=F32
        )
        return 0

    lax.fori_loop(0, pixels // CHUNK, step, 0)
    blocks, offset = bands(width)
    out_ref[...] = jnp.zeros_like(out_ref)
    for i, j, height, at in blocks:
        wide = min(LANES, width - j * LANES)
        out_ref[at : at + height, :wide] = acc[
            i * LANES : i * LANES + height, j * LANES : j * LANES + wide
        ]
    moment = acc[width : width + 1] + acc[width + 1 : width + 2]
    moment = moment + acc[width + 2 : width + 3]
    for j in range(pl.cdiv(width, LANES)):
        wide = min(LANES, width - j * LANES)
        out_ref[offset + j : offset + j + 1, :wide] = moment[
            :, j * LANES : j * LANES + wide
        ]


def small_inverse(p):
    n = len(p)
    for k in range(n):
        d = 1.0 / p[k][k]
        row = [d if j == k else p[k][j] * d for j in range(n)]
        new = []
        for i in range(n):
            if i == k:
                new.append(row)
            else:
                new.append(
                    [
                        -p[i][k] * d if j == k else p[i][j] - p[i][k] * row[j]
                        for j in range(n)
                    ]
                )
        p = new
    return p


def block_inverse(block, pivots, group=8):
    tiles = [block[8 * g : 8 * g + 8] for g in range(LANES // 8)]
    lane = lax.broadcasted_iota(jnp.int32, (8, LANES), 1)
    line = lax.broadcasted_iota(jnp.int32, (8, LANES), 0)
    for k in range(0, pivots, group):
        g, r = divmod(k, 8)
        cols = [
            [
                jnp.broadcast_to(t[:, k + j : k + j + 1], (8, LANES))
                for t in tiles
            ]
            for j in range(group)
        ]
        small = [
            [cols[j][g][r + i : r + i + 1] for j in range(group)]
            for i in range(group)
        ]
        small = small_inverse(small)
        rows = []
        for i in range(group):
            old = tiles[g][r + i : r + i + 1]
            old = jnp.where((lane[:1] >= k) & (lane[:1] < k + group), 0.0, old)
            rows.append(jnp.where(lane[:1] == k + i, 1.0, old))
        new_rows = []
        for i in range(group):
            total = small[i][0] * rows[0]
            for j in range(1, group):
                total = total + small[i][j] * rows[j]
            new_rows.append(jnp.broadcast_to(total, (8, LANES)))
        keep = (lane < k) | (lane >= k + group)
        for t in range(LANES // 8):
            value = jnp.where(keep, tiles[t], 0.0)
            for j in range(group):
                value = value - cols[j][t] * new_rows[j]
            if t == g:
                for i in range(group):
                    value = jnp.where(line == r + i, new_rows[i], value)
            tiles[t] = value
    return jnp.concatenate(tiles, 0)


def dot32(a, b):
    return jnp.dot(
        a, b, precision=lax.Precision.HIGHEST, preferred_element_type=F32
    )


def solve_kernel(
    packed_ref,
    feats_ref,
    index_ref,
    yield_ref,
    fitted_ref,
    spread_ref,
    resid_ref,
    system,
    base,
    high_ref,
    low_ref,
    fit,
):
    width, pixels = feats_ref.shape
    count = pl.cdiv(width, LANES)
    size = count * LANES
    blocks, offset = bands(width)
    scale = 1.0 / pixels
    line = lax.broadcasted_iota(jnp.int32, (LANES, LANES), 0)
    lane = lax.broadcasted_iota(jnp.int32, (LANES, LANES), 1)
    for i, j, height, at in blocks:
        value = packed_ref[at : at + height] * scale
        if height < LANES:
            value = jnp.concatenate(
                [value, jnp.zeros((LANES - height, LANES), F32)], 0
            )
        if i == j:
            diagonal = jnp.where(line < height, ridge_term, 1.0)
            value = value + jnp.where(line == lane, diagonal, 0.0)
        system[i * LANES : (i + 1) * LANES, j * LANES : (j + 1) * LANES] = value
        if i != j:
            system[j * LANES : (j + 1) * LANES, i * LANES : (i + 1) * LANES] = value.T

    base[...] = system[...]
    column = lax.broadcasted_iota(jnp.int32, (LANES, size), 1)
    wide_line = lax.broadcasted_iota(jnp.int32, (LANES, size), 0)

    def eliminate(k, pivots):
        at = k * LANES if isinstance(k, int) else pl.multiple_of(k * LANES, LANES)
        here = pl.ds(at, LANES)
        inverse = block_inverse(system[here, here], pivots)
        inside = (column >= at) & (column < at + LANES)
        unit = jnp.where(column == wide_line + at, 1.0, 0.0)
        right = dot32(inverse, jnp.where(inside, unit, system[here, :]))
        left = system[:, here]
        system[:, here] = jnp.zeros_like(left)
        system[...] -= dot32(left, right)
        system[here, :] = right

    full = width // LANES

    def body(k, _):
        eliminate(k, LANES)
        return 0

    lax.fori_loop(0, full, body, 0)
    if width % LANES:
        eliminate(full, width % LANES)

    rhs = jnp.concatenate(
        [packed_ref[offset + j : offset + j + 1] for j in range(count)], 1
    )
    rhs = jnp.broadcast_to(rhs * scale, (8, size))
    beta = dot32(rhs, system[...])
    beta = beta + dot32(rhs - dot32(beta, base[...]), system[...])
    beta = beta[:1, :width]
    inverse = system[:width, :width]
    upper = inverse.astype(BF16)
    a, b, d = (p.astype(F32) for p in split3(beta))
    row16 = lax.broadcasted_iota(jnp.int32, (16, width), 0)
    extra = jnp.where(row16 == 0, a, jnp.where(row16 == 1, b, jnp.where(row16 == 2, d, 0.0)))
    high_ref[...] = jnp.concatenate([upper, extra.astype(BF16)], 0)
    low_ref[...] = (inverse - upper.astype(F32)).astype(BF16)

    def step(c, _):
        at = pl.multiple_of(c * CHUNK, CHUNK)
        feats = feats_ref[:, pl.ds(at, CHUNK)]
        first = jnp.dot(high_ref[...], feats, preferred_element_type=F32)
        second = jnp.dot(low_ref[...], feats, preferred_element_type=F32)
        total = (first[:width] + second) * feats.astype(F32)
        spread_ref[:, pl.ds(at, CHUNK)] = jnp.sum(total, 0, keepdims=True) / width
        fitted = first[width : width + 1] + (
            first[width + 1 : width + 2] + first[width + 2 : width + 3]
        )
        fitted_ref[:, pl.ds(at, CHUNK)] = fitted
        for s in range(CHUNK // LANES):
            fit[pl.ds(c * (CHUNK // LANES) + s, 1), :] = fitted[
                :, s * LANES : (s + 1) * LANES
            ]
        return 0

    lax.fori_loop(0, pixels // CHUNK, step, 0)

    rows = pixels // LANES
    high, low = one_hots(index_ref[...], rows)
    low = jnp.where(low, 1.0, 0.0).astype(BF16)
    table = jnp.concatenate(split3(fit[...]), 0)
    found = jnp.dot(table, low, preferred_element_type=F32)
    found = found[:rows] + (found[rows : 2 * rows] + found[2 * rows :])
    value = jnp.sum(jnp.where(high, found, 0.0), 0, keepdims=True)
    resid_ref[...] = yield_ref[...] - value


PARAMS = pltpu.CompilerParams(vmem_limit_bytes=48 * 1024 * 1024)


def segments(index, yields, mask):
    shape = jax.ShapeDtypeStruct(mask.shape, F32)
    return pl.pallas_call(
        segment_kernel,
        out_shape=(shape, shape),
        compiler_params=PARAMS,
        cost_estimate=pl.CostEstimate(
            flops=2 * 128 * 128 * index.shape[1],
            bytes_accessed=16 * index.shape[1],
            transcendentals=0,
        ),
        name="segments",
    )(index, yields, mask)


def grams(feats, weight, product):
    width, pixels = feats.shape
    rows = bands(width)[1] + 8 * pl.cdiv(pl.cdiv(width, LANES), 8)
    return pl.pallas_call(
        gram_kernel,
        out_shape=jax.ShapeDtypeStruct((rows, LANES), F32),
        scratch_shapes=[pltpu.VMEM((width + 16, width), F32)],
        compiler_params=PARAMS,
        name="grams",
    )(feats, weight, product)


def solves(packed, feats, index, yields):
    width, pixels = feats.shape
    size = pl.cdiv(width, LANES) * LANES
    shape = jax.ShapeDtypeStruct((1, pixels), F32)
    return pl.pallas_call(
        solve_kernel,
        out_shape=(shape, shape, jax.ShapeDtypeStruct(yields.shape, F32)),
        scratch_shapes=[
            pltpu.VMEM((size, size), F32),
            pltpu.VMEM((size, size), F32),
            pltpu.VMEM((width + 16, width), BF16),
            pltpu.VMEM((width, width), BF16),
            pltpu.VMEM((pixels // LANES, LANES), F32),
        ],
        compiler_params=PARAMS,
        name="solves",
    )(packed, feats, index, yields)


def window_kernel(shape, own_ref, out_ref, landed, middle, send_sem, recv_sem):
    tiles, cols, dates = shape
    row = lax.axis_index("tiles")
    col = lax.axis_index("cols") * dates + lax.axis_index("dates")
    total = own_ref.shape[0]
    step = -(-total // (8 * PIECES)) * 8
    pieces = [pl.ds(at, min(step, total - at)) for at in range(0, total, step)]

    def place(c):
        return {"cols": c // dates, "dates": c % dates}

    links = (
        (row < tiles - 1, lambda: {"tiles": row + 1}, row > 0, lambda: {"tiles": row - 1}),
        (row > 0, lambda: {"tiles": row - 1}, row < tiles - 1, lambda: {"tiles": row + 1}),
        (col < cols * dates - 1, lambda: place(col + 1), col > 0, lambda: place(col - 1)),
        (col > 0, lambda: place(col - 1), col < cols * dates - 1, lambda: place(col + 1)),
    )

    def copy(d, i, source, device):
        return pltpu.make_async_remote_copy(
            src_ref=source.at[pieces[i]],
            dst_ref=landed.at[d, pieces[i]],
            send_sem=send_sem.at[d, i],
            recv_sem=recv_sem.at[d, i],
            device_id=device,
            device_id_type=pl.DeviceIdType.MESH,
        )

    barrier = pltpu.get_barrier_semaphore()
    for there, target, _, _ in links:

        @pl.when(there)
        def _(target=target):
            pl.semaphore_signal(
                barrier, inc=1, device_id=target(), device_id_type=pl.DeviceIdType.MESH
            )

    peers = sum(there.astype(jnp.int32) for there, _, _, _ in links)
    pl.semaphore_wait(barrier, peers)

    def send(d, i, source):
        there, target, _, _ = links[d]

        @pl.when(there)
        def _():
            copy(d, i, source, target()).start()

    def receive(d, i, source, into):
        _, _, there, origin = links[d]

        @pl.when(there)
        def _():
            copy(d, i, source, origin()).wait_recv()
            into[pieces[i]] += 0.5 * landed[d, pieces[i]]

    count = len(pieces)
    for i in range(count):
        send(0, i, own_ref)
        send(1, i, own_ref)
    for i in range(count):
        middle[pieces[i]] = own_ref[pieces[i]]
        receive(0, i, own_ref, middle)
        receive(1, i, own_ref, middle)
        send(2, i, middle)
        send(3, i, middle)
    for i in range(count):
        out_ref[pieces[i]] = middle[pieces[i]]
        receive(2, i, middle, out_ref)
        receive(3, i, middle, out_ref)
    for i in range(count):
        for d in range(4):
            there, target, _, _ = links[d]

            @pl.when(there)
            def _(d=d, i=i, target=target):
                copy(d, i, own_ref if d < 2 else middle, target()).wait_send()


def window(packed):
    shape = tuple(lax.axis_size(name) for name in ("tiles", "cols", "dates"))
    in_vmem = pl.BlockSpec(memory_space=pltpu.VMEM)
    return pl.pallas_call(
        functools.partial(window_kernel, shape),
        out_shape=jax.ShapeDtypeStruct(packed.shape, F32),
        in_specs=[in_vmem],
        out_specs=in_vmem,
        scratch_shapes=[
            pltpu.VMEM((4,) + packed.shape, F32),
            pltpu.VMEM(packed.shape, F32),
            pltpu.SemaphoreType.DMA((4, PIECES)),
            pltpu.SemaphoreType.DMA((4, PIECES)),
        ],
        compiler_params=pltpu.CompilerParams(
            collective_id=0,
            has_side_effects=True,
            vmem_limit_bytes=48 * 1024 * 1024,
        ),
        name="window",
    )(packed)


def on_device(imagery, pixel_mask, point_pixel, point_yield):
    whole = lax.all_to_all(imagery, "dates", split_axis=1, concat_axis=2, tiled=True)
    feats = whole[0, 0]
    pixels = feats.shape[1]
    index = point_pixel[0]
    yields = point_yield[0]
    mask = pixel_mask.reshape(pixels // LANES, LANES)
    weight, product = segments(index, yields, mask)
    packed = grams(feats, weight, product)
    packed = window(packed)
    fitted, spread, resid = solves(packed, feats, index, yields)
    return (fitted[None], spread[None], resid[None])


def solution(mesh):
    features = P(("groups", "tiles"), "cols", "dates", None)
    points = P(("groups", "tiles"), ("cols", "dates"), None)
    return jax.shard_map(
        on_device,
        mesh=mesh,
        in_specs=(features, points, points, points),
        out_specs=(points, points, points),
        check_vma=False,
    )
```

profile of v0, /device:TPU:0, one launch (start us, length us, event | category | flops | bytes accessed | tf_op | source)
XLA Modules:
  0.0 106.0 jit_solution(14838098726281168763)
XLA Ops:
  0.6 0.0 copy-start
  0.6 4.2 %all-to-all-start = ((bf16[1,2,216,4096]{3,2,0,1:T(8,128)(2,1)}), bf16[1,2,216,4096]{3,2,0,1:T(8,128)(2,1)S(1)}, u32[]{:S(2)}, u32[]{:S(2)}) async-start(bf16[1,2,216,4096]{3,2,0,1:T(8,128)(2,1)} %bitcast.15), calls=%async_computation | async-start | bytes 7077888 | tf_op jit(solution)/shard_map/all_to_all | solution.py:423
  4.9 0.0 copy-done
  4.9 0.0 copy-start.1
  4.9 0.7 copy-done.1
  5.6 0.0 copy-start.7
  5.6 0.7 copy-done.7
  6.3 0.5 segments.1
  6.8 0.0 copy-start.3
  6.8 0.6 copy-done.3
  7.4 0.0 copy-start.5
  7.4 0.6 copy-done.5
  8.0 38.4 %all-to-all-done = bf16[1,2,216,4096]{3,2,0,1:T(8,128)(2,1)S(1)} async-done(((bf16[1,2,216,4096]{3,2,0,1:T(8,128)(2,1)}), bf16[1,2,216,4096]{3,2,0,1:T(8,128)(2,1)S(1)}, u32[]{:S(2)}, u32[]{:S(2)}) %all-to-all-start) | async-done | bytes 3538976 | tf_op jit(solution)/shard_map/all_to_all | solution.py:423
  46.4 0.0 copy-start.2
  46.4 0.0 copy-start.4
  46.4 0.7 copy-done.4
  47.1 0.0 copy-start.6
  47.1 0.7 copy-done.6
  47.9 3.5 %grams.1.own_ref = f32[968,128]{1,0:T(8,128)S(1)} custom-call(bf16[432,4096]{1,0:T(8,128)(2,1)S(1)} %bitcast.8, f32[32,128]{1,0:T(8,128)S(1)} %copy-done.4, f32[32,128]{1,0:T(8,128)S(1)} %copy-done.6), custom_call_target="tpu_custom_call" | custom-call | tf_op jit(solution)/shard_map/grams/pallas_call | solution.py:293
  51.4 22.7 %window.1.packed_ref = f32[968,128]{1,0:T(8,128)S(1)} custom-call(f32[968,128]{1,0:T(8,128)S(1)} %grams.1.own_ref), custom_call_target="tpu_custom_call" | custom-call | tf_op jit(solution)/shard_map/window/pallas_call | solution.py:402
  74.1 0.0 copy-done.2
  74.1 31.9 %solves.1 = (f32[1,4096]{1,0:T(1,128)}, f32[1,4096]{1,0:T(1,128)}, f32[1,4096]{1,0:T(1,128)}) custom-call(f32[968,128]{1,0:T(8,128)S(1)} %window.1.packed_ref, bf16[432,4096]{1,0:T(8,128)(2,1)S(1)} %bitcast.9, s32[1,4096]{1,0:T(1,128)S(1)} %bitcast.11, f32[1,4096]{1,0:T(1,128)S(1)} %bitcast.13), custom_call_target="tpu_custom_call" | custom-call | tf_op jit(solution)/shard_map/solves/pallas_call | solution.py:306
Async XLA Ops:
  0.6 4.2 %copy-start = (s32[1,1,4096]{2,1,0:T(1,128)S(1)}, s32[1,1,4096]{2,1,0:T(1,128)}, u32[]{:S(2)}) copy-start(s32[1,1,4096]{2,1,0:T(1,128)} %param.6) | copy-start | bytes 49156
  0.6 45.8 %all-to-all-start = ((bf16[1,2,216,4096]{3,2,0,1:T(8,128)(2,1)}), bf16[1,2,216,4096]{3,2,0,1:T(8,128)(2,1)S(1)}, u32[]{:S(2)}, u32[]{:S(2)}) async-start(bf16[1,2,216,4096]{3,2,0,1:T(8,128)(2,1)} %bitcast.15), calls=%async_computation | async-start | bytes 7077888 | tf_op jit(solution)/shard_map/all_to_all | solution.py:423
  4.9 0.7 copy-start.1
  5.6 0.7 copy-start.7
  6.8 0.6 copy-start.3
  7.4 0.6 copy-start.5
  46.4 27.7 %copy-start.2 = (f32[1,1,4096]{2,1,0:T(1,128)S(1)}, f32[1,1,4096]{2,1,0:T(1,128)}, u32[]{:S(2)}) copy-start(f32[1,1,4096]{2,1,0:T(1,128)} %param.7) | copy-start | bytes 49156
  46.4 0.7 copy-start.4
  47.1 0.7 copy-start.6
where the time goes:
time: 107 us; the launch traced here: 106 us
  Pallas kernels  58.6 us (55%)
  waiting for transfers between devices  38.4 us (36%)
  starting transfers between devices  4.22 us (4%)
  local copies, waits for them, and re-layouts  4.1 us (4%)
    all_to_all x1, waiting for transfers between devices, on_device(): lax.all_to_all(imagery, 'dates', split_axis=1, concat_axis=2, tiled=True)  38.4 us
    pallas_call x1, Pallas kernels, solves(): pl.pallas_call(solve_kernel, out_shape=(shape, shape, jax.ShapeDtypeStruc...  31.9 us
    pallas_call x1, Pallas kernels, window(): pl.pallas_call(functools.partial(window_kernel, shape), out_shape=jax.Sha...  22.7 us
    all_to_all x1, starting transfers between devices, on_device(): lax.all_to_all(imagery, 'dates', split_axis=1, concat_axis=2, tiled=True)  4.22 us
    unnamed x16, local copies, waits for them, and re-layouts  4.1 us
    pallas_call x1, Pallas kernels, grams(): pl.pallas_call(gram_kernel, out_shape=jax.ShapeDtypeStruct((rows, LANES),...  3.52 us
  transfers between devices with their start and end apart: 1, of which 1 were waited for; matrix products, arithmetic and copies ran while one was open for 0% of the time, Pallas kernels for 0%

commit v1 on v0

--- a/solution.py
+++ b/solution.py
@@ -159,9 +159,12 @@
     return jnp.concatenate(tiles, 0)
 
 
-def dot32(a, b):
-    return jnp.dot(
-        a, b, precision=lax.Precision.HIGHEST, preferred_element_type=F32
+NN = (((1,), (0,)), ((), ()))
+
+
+def dot32(a, b, dims=NN):
+    return lax.dot_general(
+        a, b, dims, precision=lax.Precision.HIGHEST, preferred_element_type=F32
     )
 
 
@@ -433,11 +436,524 @@
     return (fitted[None], spread[None], resid[None])
 
 
+def step_rows(full, k):
+    return 128 if k < full else 64
+
+
+def payload_rows(full, k):
+    return (128 if k < full else 48) * (k + 1) + 8
+
+
+def payload_starts(full):
+    starts, at = [], 0
+    for k in range(full + 1):
+        starts.append(at)
+        at += payload_rows(full, k)
+    return starts, at
+
+
+def squeeze(block):
+    return jnp.concatenate([block[0:24], block[32:56]], 0)
+
+
+def stretch(block):
+    gap = jnp.zeros((8, block.shape[1]), block.dtype)
+    return jnp.concatenate([block[0:24], gap, block[24:48], gap], 0)
+
+
+def factor8(small):
+    plane = lax.broadcasted_iota(jnp.int32, small.shape, 0)
+    line = lax.broadcasted_iota(jnp.int32, small.shape, 1)
+    lower = jnp.where(plane == line, 1.0, 0.0)
+    pivots = jnp.zeros(small.shape[1:], F32)
+    for p in range(8):
+        pivot = small[p : p + 1, p : p + 1]
+        pivots = jnp.where(line[0] == p, pivot[0], pivots)
+        lower = jnp.where((line == p) & (plane < p), small, lower)
+        d = 1.0 / pivot
+        row = small[:, p : p + 1] * d
+        column = small[p : p + 1]
+        rest = small - column * row
+        rest = jnp.where(plane == p, -column * d, rest)
+        row = jnp.where(plane[:, :1] == p, d, row)
+        small = jnp.where(line == p, row, rest)
+    return small, lower, lax.rsqrt(pivots)
+
+
+def mix(planes, lines):
+    total = planes[0] * lines[0:1]
+    for j in range(1, 8):
+        total = total + planes[j] * lines[j : j + 1]
+    return total
+
+
+def block_factor(block, groups):
+    rows = block.shape[0]
+    lane = lax.broadcasted_iota(jnp.int32, (8, LANES), 1)
+    line = lax.broadcasted_iota(jnp.int32, (8, LANES), 0)
+    result = [jnp.zeros((8, LANES), F32)] * (rows // 8)
+    below, first = block, 0
+    for g in groups:
+        k = 8 * g
+        below = below[k - first :]
+        top = below[:8]
+        small = jnp.stack(
+            [jnp.broadcast_to(top[:, k + j : k + j + 1], (8, LANES)) for j in range(8)]
+        )
+        small, lower, root = factor8(small)
+        inside = (lane >= k) & (lane < k + 8)
+        top = jnp.where(inside, jnp.where(lane == line + k, 1.0, 0.0), top)
+        result[g] = jnp.where(lane < k + 8, mix(lower, top) * root, 0.0)
+        below = below[8:]
+        first = k + 8
+        if below.shape[0]:
+            new = mix(small, top)
+            cols = [below[:, k + j : k + j + 1] for j in range(8)]
+            keep = (lane[:1] < k) | (lane[:1] >= k + 8)
+            below = jnp.where(keep, below, 0.0)
+            for j in range(8):
+                below = below - cols[j] * new[j : j + 1]
+    return jnp.concatenate(result, 0)
+
+
+def split2(x):
+    high = x.astype(BF16)
+    return high, (x - high.astype(F32)).astype(BF16)
+
+
+def fused_kernel(
+    tiles,
+    img,
+    index_hbm,
+    yield_hbm,
+    mask_hbm,
+    fitted_ref,
+    spread_ref,
+    resid_ref,
+    feats,
+    whole,
+    tail,
+    index_ref,
+    yield_ref,
+    mask_ref,
+    weight_rows,
+    product_rows,
+    low_ref,
+    acc,
+    own,
+    middle,
+    outgoing,
+    landed,
+    inverse,
+    high_r,
+    low_r,
+    rhs_ref,
+    z_ref,
+    fit8,
+    spread8,
+    fit,
+    local_sem,
+    bulk_send,
+    bulk_recv,
+    z_send,
+    z_recv,
+    core_send,
+    core_recv,
+    x_send,
+    x_recv,
+):
+    half, pixels = img.shape[2:]
+    full = half // 64
+    steps = full + 1
+    rows = pixels // LANES
+    scale = 1.0 / pixels
+    starts, _ = payload_starts(full)
+    mesh_ids = pl.DeviceIdType.MESH
+
+    z = lax.axis_index("tiles")
+    c = lax.axis_index("cols")
+    d = lax.axis_index("dates")
+    across = {"dates": 1 - d}
+    core = {"cols": 1 - c}
+    up, down = {"tiles": z + 1}, {"tiles": z - 1}
+    has_up, has_down = z < tiles - 1, z > 0
+    joins = c == d
+
+    def place(k, s):
+        if k < full:
+            return pl.multiple_of(128 * k + 64 * s, 16)
+        return pl.multiple_of(128 * full + 32 * s, 16)
+
+    height = [64] * full + [16]
+    source_at = [64 * k for k in range(steps)]
+
+    local = [
+        pltpu.make_async_copy(index_hbm.at[0], index_ref, local_sem.at[0]),
+        pltpu.make_async_copy(yield_hbm.at[0], yield_ref, local_sem.at[1]),
+        pltpu.make_async_copy(mask_hbm, mask_ref, local_sem.at[2]),
+        pltpu.make_async_copy(img.at[0], whole, local_sem.at[3]),
+    ]
+    for k in range(steps):
+        local.append(
+            pltpu.make_async_copy(
+                img.at[0, d, pl.ds(source_at[k], height[k])],
+                feats.at[pl.ds(place(k, d), height[k])],
+                local_sem.at[4 + k],
+            )
+        )
+    for copy in local:
+        copy.start()
+
+    barrier = pltpu.get_barrier_semaphore()
+    peers = ((has_up, up), (has_down, down), (None, core), (None, across))
+    for there, target in peers:
+
+        def greet(target=target):
+            pl.semaphore_signal(
+                barrier, inc=1, device_id=target, device_id_type=mesh_ids
+            )
+
+        if there is None:
+            greet()
+        else:
+            pl.when(there)(greet)
+    pl.semaphore_wait(barrier, 2 + has_up.astype(jnp.int32) + has_down.astype(jnp.int32))
+
+    bulk = []
+    for k in range(steps):
+        bulk.append(
+            pltpu.make_async_remote_copy(
+                src_ref=img.at[0, 1 - d, pl.ds(source_at[k], height[k])],
+                dst_ref=feats.at[pl.ds(place(k, d), height[k])],
+                send_sem=bulk_send.at[k],
+                recv_sem=bulk_recv.at[k],
+                device_id=across,
+                device_id_type=mesh_ids,
+            )
+        )
+    bulk.append(
+        pltpu.make_async_remote_copy(
+            src_ref=tail.at[1 - d],
+            dst_ref=feats.at[pl.ds(pl.multiple_of(128 * full + 32 * d + 16, 16), 16)],
+            send_sem=bulk_send.at[steps],
+            recv_sem=bulk_recv.at[steps],
+            device_id=across,
+            device_id_type=mesh_ids,
+        )
+    )
+    for k in range(steps):
+        bulk[k].start()
+
+    for copy in local[:4]:
+        copy.wait()
+    for s in range(2):
+        end = whole[s][half - 8 : half]
+        tail[s] = jnp.concatenate([end, jnp.zeros_like(end)], 0)
+    bulk[steps].start()
+    feats[pl.ds(pl.multiple_of(128 * full + 32 * d + 16, 16), 16), :] = tail[d]
+
+    high, low = one_hots(index_ref[...], rows)
+    low = jnp.where(low, 1.0, 0.0).astype(BF16)
+    low_ref[...] = low
+    parts = [jnp.where(high, 1.0, 0.0).astype(BF16)]
+    for piece in split3(yield_ref[...]):
+        parts.append(jnp.where(high, piece.astype(F32), 0.0).astype(BF16))
+    sums = lax.dot_general(
+        jnp.concatenate(parts, 0), low, NT, preferred_element_type=F32
+    )
+    counts = sums[:rows]
+    totals = sums[rows : 2 * rows] + sums[2 * rows : 3 * rows] + sums[3 * rows :]
+    weight = jnp.where(counts > 0, mask_ref[...].astype(F32), 0.0)
+    product = weight * (totals / jnp.maximum(counts, 1.0))
+    pa, pb, pc = (p.astype(F32) for p in split3(product))
+    line16 = lax.broadcasted_iota(jnp.int32, (16, LANES), 0)
+    for r in range(rows):
+        at = slice(r * LANES, (r + 1) * LANES)
+        weight_rows[:, at] = jnp.broadcast_to(weight[r : r + 1], (16, LANES)).astype(BF16)
+        extra = jnp.where(
+            line16 == 0,
+            pa[r : r + 1],
+            jnp.where(
+                line16 == 1,
+                pb[r : r + 1],
+                jnp.where(line16 == 2, pc[r : r + 1], 0.0),
+            ),
+        )
+        product_rows[:, at] = extra.astype(BF16)
+
+    acc[...] = jnp.zeros_like(acc)
+    inverse[...] = jnp.zeros_like(inverse)
+    fit8[...] = jnp.zeros_like(fit8)
+    spread8[...] = jnp.zeros_like(spread8)
+
+    def payload(k):
+        return pl.ds(starts[k], payload_rows(full, k))
+
+    def z_copy(way, k, target):
+        return pltpu.make_async_remote_copy(
+            src_ref=own.at[payload(k)],
+            dst_ref=landed.at[way, payload(k)],
+            send_sem=z_send.at[way, k],
+            recv_sem=z_recv.at[way, k],
+            device_id=target,
+            device_id_type=mesh_ids,
+        )
+
+    def core_copy(k):
+        return pltpu.make_async_remote_copy(
+            src_ref=middle.at[payload(k)],
+            dst_ref=landed.at[2, payload(k)],
+            send_sem=core_send.at[k],
+            recv_sem=core_recv.at[k],
+            device_id=core,
+            device_id_type=mesh_ids,
+        )
+
+    def x_copy(k):
+        return pltpu.make_async_remote_copy(
+            src_ref=outgoing.at[payload(k)],
+            dst_ref=landed.at[3, payload(k)],
+            send_sem=x_send.at[k],
+            recv_sem=x_recv.at[k],
+            device_id=across,
+            device_id_type=mesh_ids,
+        )
+
+    def gram(k):
+        count = step_rows(full, k)
+        base, end = 128 * k, 128 * k + count
+        local[4 + k].wait()
+        bulk[k].wait_recv()
+        if k == full:
+            bulk[steps].wait_recv()
+        acc[: count + 16, :end] = jnp.zeros((count + 16, end), F32)
+
+        def chunk(i, _):
+            at = pl.ds(pl.multiple_of(i * CHUNK, CHUNK), CHUNK)
+            weights = jnp.concatenate([weight_rows[:, at]] * (count // 16), 0)
+            left = jnp.concatenate(
+                [feats[base:end, at] * weights, product_rows[:, at]], 0
+            )
+            acc[: count + 16, :end] += lax.dot_general(
+                left, feats[:end, at], NT, preferred_element_type=F32
+            )
+            return 0
+
+        lax.fori_loop(0, pixels // CHUNK, chunk, 0)
+        at = starts[k]
+        for j in range(k + 1):
+            block = acc[:count, 128 * j : 128 * j + 128]
+            if k == full:
+                block = squeeze(block)
+            own[at : at + block.shape[0]] = block
+            at += block.shape[0]
+        moment = acc[count : count + 1, base : base + 128]
+        moment = moment + acc[count + 1 : count + 2, base : base + 128]
+        moment = moment + acc[count + 2 : count + 3, base : base + 128]
+        own[at : at + 8] = jnp.broadcast_to(moment, (8, LANES))
+        pl.when(has_up)(lambda: z_copy(0, k, up).start())
+        pl.when(has_down)(lambda: z_copy(1, k, down).start())
+
+    def z_join(k):
+        at = payload(k)
+        middle[at] = own[at]
+
+        @pl.when(has_down)
+        def _():
+            z_copy(0, k, down).wait_recv()
+            middle[at] += 0.5 * landed[0, at]
+
+        @pl.when(has_up)
+        def _():
+            z_copy(1, k, up).wait_recv()
+            middle[at] += 0.5 * landed[1, at]
+
+        @pl.when(jnp.logical_not(joins))
+        def _():
+            core_copy(k).start()
+            outgoing[at] = middle[at]
+
+        @pl.when(joins)
+        def _():
+            core_copy(k).wait_recv()
+            outgoing[at] = middle[at] + landed[2, at]
+
+        x_copy(k).start()
+
+    def solve(k):
+        at = payload(k)
+        x_copy(k).wait_recv()
+        count = step_rows(full, k)
+        base = 128 * k
+        window = (middle[at] + 0.5 * landed[3, at]) * scale
+        step = 128 if k < full else 48
+        blocks = [window[j * step : (j + 1) * step] for j in range(k + 1)]
+        if k == full:
+            blocks = [stretch(block) for block in blocks]
+        rhs_ref[:, base : base + 128] = window[(k + 1) * step : (k + 1) * step + 8]
+        lane = lax.broadcasted_iota(jnp.int32, (count, LANES), 1)
+        line = lax.broadcasted_iota(jnp.int32, (count, LANES), 0)
+        pivot = blocks[k] + jnp.where(lane == line, ridge_term, 0.0)
+        if k:
+            left = jnp.concatenate(blocks[:k], 1)
+            known = inverse[:base, :base]
+            factor = dot32(left, known, NT)
+            drop = dot32(factor, factor, NT)
+            coupling = dot32(factor, known)
+            if count < LANES:
+                drop = jnp.concatenate(
+                    [drop, jnp.zeros((count, LANES - count), F32)], 1
+                )
+            pivot = pivot - drop
+        groups = range(16) if k < full else (0, 1, 2, 4, 5, 6)
+        lower = block_factor(pivot, groups)
+        if k:
+            lower = jnp.concatenate([-dot32(lower[:, :count], coupling), lower], 1)
+        z_ref[:count] = jnp.sum(
+            lower * rhs_ref[:1, : base + 128], 1, keepdims=True
+        )
+        high, low = split2(lower)
+        high_r[:count, : base + 128] = high
+        low_r[:count, : base + 128] = low
+        if k < full:
+            inverse[base : base + count, : base + 128] = lower
+
+    def spread(k):
+        count = step_rows(full, k)
+        end = 128 * k + count
+        last = k == full
+
+        def chunk(i, _):
+            at = pl.ds(pl.multiple_of(i * CHUNK, CHUNK), CHUNK)
+            part = feats[:end, at]
+            value = jnp.dot(
+                high_r[:count, :end], part, preferred_element_type=F32
+            ) + jnp.dot(low_r[:count, :end], part, preferred_element_type=F32)
+            square = (value * value).reshape(count // 8, 8, CHUNK)
+            linear = (value * z_ref[:count]).reshape(count // 8, 8, CHUNK)
+            square = spread8[:, at] + jnp.sum(square, 0)
+            linear = fit8[:, at] + jnp.sum(linear, 0)
+            if last:
+                spread_ref[:, at] = jnp.sum(square, 0, keepdims=True) / (2 * half)
+                fitted = jnp.sum(linear, 0, keepdims=True)
+                fitted_ref[:, at] = fitted
+                for s in range(CHUNK // LANES):
+                    fit[pl.ds(i * (CHUNK // LANES) + s, 1), :] = fitted[
+                        :, s * LANES : (s + 1) * LANES
+                    ]
+            else:
+                spread8[:, at] = square
+                fit8[:, at] = linear
+            return 0
+
+        lax.fori_loop(0, pixels // CHUNK, chunk, 0)
+
+    gram(0)
+    z_join(0)
+    for k in range(1, steps):
+        gram(k)
+        z_join(k)
+        solve(k - 1)
+        spread(k - 1)
+    solve(full)
+    spread(full)
+
+    high, _ = one_hots(index_ref[...], rows)
+    table = jnp.concatenate(split3(fit[...]), 0)
+    found = jnp.dot(table, low_ref[...], preferred_element_type=F32)
+    found = found[:rows] + (found[rows : 2 * rows] + found[2 * rows :])
+    value = jnp.sum(jnp.where(high, found, 0.0), 0, keepdims=True)
+    resid_ref[...] = yield_ref[...] - value
+
+    for copy in bulk:
+        copy.wait_send()
+    for k in range(steps):
+        pl.when(has_up)(lambda k=k: z_copy(0, k, up).wait_send())
+        pl.when(has_down)(lambda k=k: z_copy(1, k, down).wait_send())
+        pl.when(jnp.logical_not(joins))(lambda k=k: core_copy(k).wait_send())
+        x_copy(k).wait_send()
+
+
+def fused(imagery, index, yields, mask):
+    half, pixels = imagery.shape[2:]
+    full = half // 64
+    steps = full + 1
+    rows = payload_starts(full)[1]
+    size = 128 * steps
+    shape = jax.ShapeDtypeStruct((1, pixels), F32)
+    anywhere = pl.BlockSpec(memory_space=pl.ANY)
+    in_vmem = pl.BlockSpec(memory_space=pltpu.VMEM)
+    dma = pltpu.SemaphoreType.DMA
+    return pl.pallas_call(
+        functools.partial(fused_kernel, lax.axis_size("tiles")),
+        out_shape=(shape, shape, shape),
+        in_specs=[anywhere] * 4,
+        out_specs=(in_vmem,) * 3,
+        scratch_shapes=[
+            pltpu.VMEM((128 * full + 64, pixels), BF16),
+            pltpu.VMEM((2, half, pixels), BF16),
+            pltpu.VMEM((2, 16, pixels), BF16),
+            pltpu.VMEM((1, pixels), jnp.int32),
+            pltpu.VMEM((1, pixels), F32),
+            pltpu.VMEM((pixels // LANES, LANES), jnp.int32),
+            pltpu.VMEM((16, pixels), BF16),
+            pltpu.VMEM((16, pixels), BF16),
+            pltpu.VMEM((LANES, pixels), BF16),
+            pltpu.VMEM((LANES + 16, size), F32),
+            pltpu.VMEM((rows, LANES), F32),
+            pltpu.VMEM((rows, LANES), F32),
+            pltpu.VMEM((rows, LANES), F32),
+            pltpu.VMEM((4, rows, LANES), F32),
+            pltpu.VMEM((size, size), F32),
+            pltpu.VMEM((LANES, size), BF16),
+            pltpu.VMEM((LANES, size), BF16),
+            pltpu.VMEM((8, size), F32),
+            pltpu.VMEM((LANES, 1), F32),
+            pltpu.VMEM((8, pixels), F32),
+            pltpu.VMEM((8, pixels), F32),
+            pltpu.VMEM((pixels // LANES, LANES), F32),
+            dma((4 + steps,)),
+            dma((steps + 1,)),
+            dma((steps + 1,)),
+            dma((2, steps)),
+            dma((2, steps)),
+            dma((steps,)),
+            dma((steps,)),
+            dma((steps,)),
+            dma((steps,)),
+        ],
+        compiler_params=pltpu.CompilerParams(
+            collective_id=1,
+            has_side_effects=True,
+            vmem_limit_bytes=56 * 1024 * 1024,
+        ),
+        name="fused",
+    )(imagery, index, yields, mask)
+
+
+def on_device_fused(imagery, pixel_mask, point_pixel, point_yield):
+    pixels = imagery.shape[3]
+    mask = pixel_mask.reshape(pixels // LANES, LANES)
+    fitted, spread, resid = fused(imagery, point_pixel, point_yield, mask)
+    return (fitted[None], spread[None], resid[None])
+
+
 def solution(mesh):
     features = P(("groups", "tiles"), "cols", "dates", None)
     points = P(("groups", "tiles"), ("cols", "dates"), None)
+    sizes = dict(mesh.shape)
+
+    def body(imagery, pixel_mask, point_pixel, point_yield):
+        pairs = sizes["cols"] == 2 and sizes["dates"] == 2
+        one_tile = imagery.shape[:2] == (1, 2)
+        if pairs and one_tile and imagery.shape[2] % 64 == 24:
+            run = on_device_fused
+        else:
+            run = on_device
+        return run(imagery, pixel_mask, point_pixel, point_yield)
+
     return jax.shard_map(
-        on_device,
+        body,
         mesh=mesh,
         in_specs=(features, points, points, points),
         out_specs=(points, points, points),

time: 107 us -> 94 us (0.88)
  waiting for transfers between devices: 38.4 us -> 0 us
  Pallas kernels: 58.6 us -> 89 us
  starting transfers between devices: 4.22 us -> 0 us
    all_to_all x1 -> x0, waiting for transfers between devices: 38.4 us -> none  [on_device(): lax.all_to_all(imagery, 'dates', split_axis=1, concat_axis=2, tiled=True)]
    pallas_call x4 -> x1, Pallas kernels: 58.6 us -> 89 us  [fused(): pl.pallas_call(functools.partial(fused_kernel, lax.axis_size('tiles')), o...]
    all_to_all x1 -> x0, starting transfers between devices: 4.22 us -> none  [on_device(): lax.all_to_all(imagery, 'dates', split_axis=1, concat_axis=2, tiled=True)]
    unnamed x16 -> x3, local copies, waits for them, and re-layouts: 4.1 us -> 3.97 us
  transfers between devices with their start and end apart: 1 -> 0, of which waited for: 1 -> 0; matrix products, arithmetic and copies ran while one was open for 0% -> 0% of each run, Pallas kernels for 0% -> 0%
where the time goes in v1:
time: 94 us; the launch traced here: 93.6 us
  Pallas kernels  89 us (95%)
  local copies, waits for them, and re-layouts  3.97 us (4%)
    pallas_call x1, Pallas kernels, fused(): pl.pallas_call(functools.partial(fused_kernel, lax.axis_size('tiles')), o...  89 us
    unnamed x3, local copies, waits for them, and re-layouts  3.97 us

profile of v1, /device:TPU:0, one launch (start us, length us, event | category | flops | bytes accessed | tf_op | source)
XLA Modules:
  0.0 93.6 jit_solution(8606783874573122899)
XLA Ops:
  0.6 89.0 %fused.1 = (f32[1,4096]{1,0:T(1,128)}, f32[1,4096]{1,0:T(1,128)}, f32[1,4096]{1,0:T(1,128)}) custom-call(bf16[1,2,216,4096]{3,2,1,0:T(8,128)(2,1)} %img.1, s32[1,1,4096]{2,1,0:T(1,128)} %index_hbm.1, f32[1,1,4096]{2,1,0:T(1,128)} %yield_hbm.1, s32[32,128]{1,0:T(8,128)} %bitcast.4), custom_call_target="tpu_custom_call" | custom-call | tf_op jit(solution)/shard_map/fused/pallas_call | solution.py:887
  89.6 1.3 %copy.10 = f32[1,1,4096]{2,1,0:T(1,128)} copy(f32[1,1,4096]{2,1,0:T(1,128)} %bitcast.7) | data formatting | bytes 32768
  90.9 1.3 %copy.11 = f32[1,1,4096]{2,1,0:T(1,128)} copy(f32[1,1,4096]{2,1,0:T(1,128)} %bitcast.6) | data formatting | bytes 32768
  92.3 1.3 %copy.12 = f32[1,1,4096]{2,1,0:T(1,128)} copy(f32[1,1,4096]{2,1,0:T(1,128)} %bitcast.5) | data formatting | bytes 32768

commit v2 on v1

--- a/solution.py
+++ b/solution.py
@@ -11,6 +11,7 @@
 LANES = 128
 CHUNK = 512
 PIECES = 8
+SPAN = 1024
 F32 = jnp.float32
 BF16 = jnp.bfloat16
 NT = (((1,), (1,)), ((), ()))
@@ -545,8 +546,7 @@
     outgoing,
     landed,
     inverse,
-    high_r,
-    low_r,
+    split_r,
     rhs_ref,
     z_ref,
     fit8,
@@ -641,15 +641,14 @@
             device_id_type=mesh_ids,
         )
     )
-    for k in range(steps):
-        bulk[k].start()
+    bulk[0].start()
+    bulk[1].start()
 
     for copy in local[:4]:
         copy.wait()
     for s in range(2):
         end = whole[s][half - 8 : half]
         tail[s] = jnp.concatenate([end, jnp.zeros_like(end)], 0)
-    bulk[steps].start()
     feats[pl.ds(pl.multiple_of(128 * full + 32 * d + 16, 16), 16), :] = tail[d]
 
     high, low = one_hots(index_ref[...], rows)
@@ -726,31 +725,35 @@
         bulk[k].wait_recv()
         if k == full:
             bulk[steps].wait_recv()
-        acc[: count + 16, :end] = jnp.zeros((count + 16, end), F32)
+        wide = count + 16
+        acc[:end, :wide] = jnp.zeros((end, wide), F32)
 
         def chunk(i, _):
-            at = pl.ds(pl.multiple_of(i * CHUNK, CHUNK), CHUNK)
+            at = pl.ds(pl.multiple_of(i * SPAN, SPAN), SPAN)
             weights = jnp.concatenate([weight_rows[:, at]] * (count // 16), 0)
             left = jnp.concatenate(
                 [feats[base:end, at] * weights, product_rows[:, at]], 0
             )
-            acc[: count + 16, :end] += lax.dot_general(
-                left, feats[:end, at], NT, preferred_element_type=F32
+            acc[:end, :wide] += lax.dot_general(
+                feats[:end, at], left, NT, preferred_element_type=F32
             )
             return 0
 
-        lax.fori_loop(0, pixels // CHUNK, chunk, 0)
+        lax.fori_loop(0, pixels // SPAN, chunk, 0)
         at = starts[k]
         for j in range(k + 1):
-            block = acc[:count, 128 * j : 128 * j + 128]
-            if k == full:
+            if k < full:
+                block = acc[128 * j : 128 * j + 128, :LANES]
+            else:
+                block = acc[128 * j : 128 * j + 128, :LANES].T
                 block = squeeze(block)
             own[at : at + block.shape[0]] = block
             at += block.shape[0]
-        moment = acc[count : count + 1, base : base + 128]
-        moment = moment + acc[count + 1 : count + 2, base : base + 128]
-        moment = moment + acc[count + 2 : count + 3, base : base + 128]
-        own[at : at + 8] = jnp.broadcast_to(moment, (8, LANES))
+        moment = acc[base : base + 128, count : count + 1]
+        moment = moment + acc[base : base + 128, count + 1 : count + 2]
+        moment = moment + acc[base : base + 128, count + 2 : count + 3]
+        moment = jnp.broadcast_to(moment, (LANES, LANES)).T
+        own[at : at + 8] = moment[:8]
         pl.when(has_up)(lambda: z_copy(0, k, up).start())
         pl.when(has_down)(lambda: z_copy(1, k, down).start())
 
@@ -779,6 +782,10 @@
             outgoing[at] = middle[at] + landed[2, at]
 
         x_copy(k).start()
+        if k + 2 < steps:
+            bulk[k + 2].start()
+        if k + 2 == full:
+            bulk[steps].start()
 
     def solve(k):
         at = payload(k)
@@ -795,10 +802,16 @@
         line = lax.broadcasted_iota(jnp.int32, (count, LANES), 0)
         pivot = blocks[k] + jnp.where(lane == line, ridge_term, 0.0)
         if k:
-            left = jnp.concatenate(blocks[:k], 1)
             known = inverse[:base, :base]
-            factor = dot32(left, known, NT)
-            drop = dot32(factor, factor, NT)
+            if k < full:
+                raised = dot32(known, jnp.concatenate(blocks[:k], 0))
+                factor = jnp.concatenate(
+                    [raised[128 * j : 128 * j + 128].T for j in range(k)], 1
+                )
+                drop = dot32(factor, raised)
+            else:
+                factor = dot32(jnp.concatenate(blocks[:k], 1), known, NT)
+                drop = dot32(factor, factor, NT)
             coupling = dot32(factor, known)
             if count < LANES:
                 drop = jnp.concatenate(
@@ -813,8 +826,8 @@
             lower * rhs_ref[:1, : base + 128], 1, keepdims=True
         )
         high, low = split2(lower)
-        high_r[:count, : base + 128] = high
-        low_r[:count, : base + 128] = low
+        split_r[:count, : base + 128] = high
+        split_r[count : 2 * count, : base + 128] = low
         if k < full:
             inverse[base : base + count, : base + 128] = lower
 
@@ -824,21 +837,22 @@
         last = k == full
 
         def chunk(i, _):
-            at = pl.ds(pl.multiple_of(i * CHUNK, CHUNK), CHUNK)
+            at = pl.ds(pl.multiple_of(i * SPAN, SPAN), SPAN)
             part = feats[:end, at]
-            value = jnp.dot(
-                high_r[:count, :end], part, preferred_element_type=F32
-            ) + jnp.dot(low_r[:count, :end], part, preferred_element_type=F32)
-            square = (value * value).reshape(count // 8, 8, CHUNK)
-            linear = (value * z_ref[:count]).reshape(count // 8, 8, CHUNK)
+            both = jnp.dot(
+                split_r[: 2 * count, :end], part, preferred_element_type=F32
+            )
+            value = both[:count] + both[count:]
+            square = (value * value).reshape(count // 8, 8, SPAN)
+            linear = (value * z_ref[:count]).reshape(count // 8, 8, SPAN)
             square = spread8[:, at] + jnp.sum(square, 0)
             linear = fit8[:, at] + jnp.sum(linear, 0)
             if last:
                 spread_ref[:, at] = jnp.sum(square, 0, keepdims=True) / (2 * half)
                 fitted = jnp.sum(linear, 0, keepdims=True)
                 fitted_ref[:, at] = fitted
-                for s in range(CHUNK // LANES):
-                    fit[pl.ds(i * (CHUNK // LANES) + s, 1), :] = fitted[
+                for s in range(SPAN // LANES):
+                    fit[pl.ds(i * (SPAN // LANES) + s, 1), :] = fitted[
                         :, s * LANES : (s + 1) * LANES
                     ]
             else:
@@ -846,15 +860,21 @@
                 fit8[:, at] = linear
             return 0
 
-        lax.fori_loop(0, pixels // CHUNK, chunk, 0)
+        lax.fori_loop(0, pixels // SPAN, chunk, 0)
 
     gram(0)
     z_join(0)
-    for k in range(1, steps):
+    for k in range(1, steps - 1):
         gram(k)
+        solve(k - 1)
         z_join(k)
-        solve(k - 1)
-        spread(k - 1)
+        if k < steps - 2:
+            spread(k - 1)
+    gram(full)
+    spread(full - 2)
+    z_join(full)
+    solve(full - 1)
+    spread(full - 1)
     solve(full)
     spread(full)
 
@@ -899,14 +919,13 @@
             pltpu.VMEM((16, pixels), BF16),
             pltpu.VMEM((16, pixels), BF16),
             pltpu.VMEM((LANES, pixels), BF16),
-            pltpu.VMEM((LANES + 16, size), F32),
+            pltpu.VMEM((size, 2 * LANES), F32),
             pltpu.VMEM((rows, LANES), F32),
             pltpu.VMEM((rows, LANES), F32),
             pltpu.VMEM((rows, LANES), F32),
             pltpu.VMEM((4, rows, LANES), F32),
             pltpu.VMEM((size, size), F32),
-            pltpu.VMEM((LANES, size), BF16),
-            pltpu.VMEM((LANES, size), BF16),
+            pltpu.VMEM((2 * LANES, size), BF16),
             pltpu.VMEM((8, size), F32),
             pltpu.VMEM((LANES, 1), F32),
             pltpu.VMEM((8, pixels), F32),

time: 94 us -> 73.6 us (0.78)
  Pallas kernels: 89 us -> 68.6 us
    pallas_call x1, Pallas kernels: 89 us -> 68.6 us  [fused(): pl.pallas_call(functools.partial(fused_kernel, lax.axis_size('tiles')), o...]
where the time goes in v2:
time: 73.6 us; the launch traced here: 73.2 us
  Pallas kernels  68.6 us (93%)
  local copies, waits for them, and re-layouts  3.97 us (5%)
    pallas_call x1, Pallas kernels, fused(): pl.pallas_call(functools.partial(fused_kernel, lax.axis_size('tiles')), o...  68.6 us
    unnamed x3, local copies, waits for them, and re-layouts  3.97 us

profile of v2, /device:TPU:0, one launch (start us, length us, event | category | flops | bytes accessed | tf_op | source)
XLA Modules:
  0.0 73.2 jit_solution(9264826266999113480)
XLA Ops:
  0.6 68.6 %fused.1 = (f32[1,4096]{1,0:T(1,128)}, f32[1,4096]{1,0:T(1,128)}, f32[1,4096]{1,0:T(1,128)}) custom-call(bf16[1,2,216,4096]{3,2,1,0:T(8,128)(2,1)} %img.1, s32[1,1,4096]{2,1,0:T(1,128)} %index_hbm.1, f32[1,1,4096]{2,1,0:T(1,128)} %yield_hbm.1, s32[32,128]{1,0:T(8,128)} %bitcast.4), custom_call_target="tpu_custom_call" | custom-call | tf_op jit(solution)/shard_map/fused/pallas_call | solution.py:907
  69.2 1.3 %copy.10 = f32[1,1,4096]{2,1,0:T(1,128)} copy(f32[1,1,4096]{2,1,0:T(1,128)} %bitcast.7) | data formatting | bytes 32768
  70.6 1.3 %copy.11 = f32[1,1,4096]{2,1,0:T(1,128)} copy(f32[1,1,4096]{2,1,0:T(1,128)} %bitcast.6) | data formatting | bytes 32768
  71.9 1.3 %copy.12 = f32[1,1,4096]{2,1,0:T(1,128)} copy(f32[1,1,4096]{2,1,0:T(1,128)} %bitcast.5) | data formatting | bytes 32768

commit v3 on v2

--- a/solution.py
+++ b/solution.py
@@ -11,7 +11,7 @@
 LANES = 128
 CHUNK = 512
 PIECES = 8
-SPAN = 1024
+SPAN = 4096
 F32 = jnp.float32
 BF16 = jnp.bfloat16
 NT = (((1,), (1,)), ((), ()))
@@ -463,29 +463,50 @@
 
 
 def factor8(small):
-    plane = lax.broadcasted_iota(jnp.int32, small.shape, 0)
-    line = lax.broadcasted_iota(jnp.int32, small.shape, 1)
-    lower = jnp.where(plane == line, 1.0, 0.0)
+    line = lax.broadcasted_iota(jnp.int32, small.shape[1:], 0)
+    lower = []
     pivots = jnp.zeros(small.shape[1:], F32)
-    for p in range(8):
-        pivot = small[p : p + 1, p : p + 1]
-        pivots = jnp.where(line[0] == p, pivot[0], pivots)
-        lower = jnp.where((line == p) & (plane < p), small, lower)
-        d = 1.0 / pivot
-        row = small[:, p : p + 1] * d
-        column = small[p : p + 1]
-        rest = small - column * row
-        rest = jnp.where(plane == p, -column * d, rest)
-        row = jnp.where(plane[:, :1] == p, d, row)
-        small = jnp.where(line == p, row, rest)
+    for p in range(0, 8, 2):
+        one, two = line == p, line == p + 1
+        first, second = small[p], small[p + 1]
+        a, b, c = first[p : p + 1], second[p : p + 1], second[p + 1 : p + 2]
+        det = a * c - b * b
+        ra = 1.0 / a
+        t = b * ra
+        pivots = jnp.where(one, a, jnp.where(two, det * ra, pivots))
+        lower = [
+            jnp.where(
+                one,
+                small[j],
+                jnp.where(two, small[j] - t * small[j][p : p + 1], lower[j]),
+            )
+            for j in range(p)
+        ]
+        lower.append(jnp.where(one, 1.0, jnp.where(two, -t, 0.0)))
+        lower.append(jnp.where(two, 1.0, 0.0))
+        r = 1.0 / det
+        ea, eb, ec = c * r, -b * r, a * r
+        left = first * ea + second * eb
+        right = first * eb + second * ec
+        left = jnp.where(one, -ea, jnp.where(two, -eb, left))
+        right = jnp.where(one, -eb, jnp.where(two, -ec, right))
+        base = jnp.where((one | two)[None], 0.0, small)
+        rest = base - (
+            left[None] * small[:, p : p + 1] + right[None] * small[:, p + 1 : p + 2]
+        )
+        parts = [rest[:p]] if p else []
+        parts.append(jnp.stack([-left, -right]))
+        if p < 6:
+            parts.append(rest[p + 2 :])
+        small = jnp.concatenate(parts, 0)
     return small, lower, lax.rsqrt(pivots)
 
 
 def mix(planes, lines):
-    total = planes[0] * lines[0:1]
-    for j in range(1, 8):
-        total = total + planes[j] * lines[j : j + 1]
-    return total
+    terms = [planes[j] * lines[j : j + 1] for j in range(8)]
+    while len(terms) > 1:
+        terms = [a + b for a, b in zip(terms[::2], terms[1::2])]
+    return terms[0]
 
 
 def block_factor(block, groups):
@@ -512,8 +533,10 @@
             cols = [below[:, k + j : k + j + 1] for j in range(8)]
             keep = (lane[:1] < k) | (lane[:1] >= k + 8)
             below = jnp.where(keep, below, 0.0)
-            for j in range(8):
-                below = below - cols[j] * new[j : j + 1]
+            for j in range(0, 8, 2):
+                below = below - (
+                    cols[j] * new[j : j + 1] + cols[j + 1] * new[j + 1 : j + 2]
+                )
     return jnp.concatenate(result, 0)
 
 
@@ -528,18 +551,19 @@
     index_hbm,
     yield_hbm,
     mask_hbm,
-    fitted_ref,
+    fit,
     spread_ref,
-    resid_ref,
+    index_out,
+    yield_out,
     feats,
     whole,
     tail,
+    tail_in,
     index_ref,
     yield_ref,
     mask_ref,
     weight_rows,
     product_rows,
-    low_ref,
     acc,
     own,
     middle,
@@ -551,7 +575,6 @@
     z_ref,
     fit8,
     spread8,
-    fit,
     local_sem,
     bulk_send,
     bulk_recv,
@@ -633,8 +656,8 @@
         )
     bulk.append(
         pltpu.make_async_remote_copy(
-            src_ref=tail.at[1 - d],
-            dst_ref=feats.at[pl.ds(pl.multiple_of(128 * full + 32 * d + 16, 16), 16)],
+            src_ref=tail,
+            dst_ref=tail_in,
             send_sem=bulk_send.at[steps],
             recv_sem=bulk_recv.at[steps],
             device_id=across,
@@ -646,14 +669,19 @@
 
     for copy in local[:4]:
         copy.wait()
-    for s in range(2):
-        end = whole[s][half - 8 : half]
-        tail[s] = jnp.concatenate([end, jnp.zeros_like(end)], 0)
-    feats[pl.ds(pl.multiple_of(128 * full + 32 * d + 16, 16), 16), :] = tail[d]
+    end = whole[1 - d][half - 8 : half]
+    tail[...] = jnp.concatenate([end[:, : pixels // 2], end[:, pixels // 2 :]], 0)
+
+    def put_tail(s, end):
+        at = pl.ds(pl.multiple_of(128 * full + 32 * s + 16, 16), 16)
+        feats[at, :] = jnp.concatenate([end, jnp.zeros_like(end)], 0)
+
+    put_tail(d, whole[d][half - 8 : half])
 
     high, low = one_hots(index_ref[...], rows)
     low = jnp.where(low, 1.0, 0.0).astype(BF16)
-    low_ref[...] = low
+    index_out[...] = index_ref[...]
+    yield_out[...] = yield_ref[...]
     parts = [jnp.where(high, 1.0, 0.0).astype(BF16)]
     for piece in split3(yield_ref[...]):
         parts.append(jnp.where(high, piece.astype(F32), 0.0).astype(BF16))
@@ -725,6 +753,8 @@
         bulk[k].wait_recv()
         if k == full:
             bulk[steps].wait_recv()
+            folded = tail_in[...]
+            put_tail(1 - d, jnp.concatenate([folded[:8], folded[8:]], 1))
         wide = count + 16
         acc[:end, :wide] = jnp.zeros((end, wide), F32)
 
@@ -850,7 +880,6 @@
             if last:
                 spread_ref[:, at] = jnp.sum(square, 0, keepdims=True) / (2 * half)
                 fitted = jnp.sum(linear, 0, keepdims=True)
-                fitted_ref[:, at] = fitted
                 for s in range(SPAN // LANES):
                     fit[pl.ds(i * (SPAN // LANES) + s, 1), :] = fitted[
                         :, s * LANES : (s + 1) * LANES
@@ -878,13 +907,6 @@
     solve(full)
     spread(full)
 
-    high, _ = one_hots(index_ref[...], rows)
-    table = jnp.concatenate(split3(fit[...]), 0)
-    found = jnp.dot(table, low_ref[...], preferred_element_type=F32)
-    found = found[:rows] + (found[rows : 2 * rows] + found[2 * rows :])
-    value = jnp.sum(jnp.where(high, found, 0.0), 0, keepdims=True)
-    resid_ref[...] = yield_ref[...] - value
-
     for copy in bulk:
         copy.wait_send()
     for k in range(steps):
@@ -901,24 +923,29 @@
     rows = payload_starts(full)[1]
     size = 128 * steps
     shape = jax.ShapeDtypeStruct((1, pixels), F32)
-    anywhere = pl.BlockSpec(memory_space=pl.ANY)
+    in_hbm = pl.BlockSpec(memory_space=pltpu.HBM)
     in_vmem = pl.BlockSpec(memory_space=pltpu.VMEM)
     dma = pltpu.SemaphoreType.DMA
     return pl.pallas_call(
         functools.partial(fused_kernel, lax.axis_size("tiles")),
-        out_shape=(shape, shape, shape),
-        in_specs=[anywhere] * 4,
-        out_specs=(in_vmem,) * 3,
+        out_shape=(
+            pltpu.VMEM((pixels // LANES, LANES), F32),
+            pltpu.VMEM((1, pixels), F32),
+            pltpu.VMEM((1, pixels), jnp.int32),
+            pltpu.VMEM((1, pixels), F32),
+        ),
+        in_specs=[in_hbm] * 4,
+        out_specs=(in_vmem,) * 4,
         scratch_shapes=[
             pltpu.VMEM((128 * full + 64, pixels), BF16),
             pltpu.VMEM((2, half, pixels), BF16),
-            pltpu.VMEM((2, 16, pixels), BF16),
+            pltpu.VMEM((16, pixels // 2), BF16),
+            pltpu.VMEM((16, pixels // 2), BF16),
             pltpu.VMEM((1, pixels), jnp.int32),
             pltpu.VMEM((1, pixels), F32),
             pltpu.VMEM((pixels // LANES, LANES), jnp.int32),
             pltpu.VMEM((16, pixels), BF16),
             pltpu.VMEM((16, pixels), BF16),
-            pltpu.VMEM((LANES, pixels), BF16),
             pltpu.VMEM((size, 2 * LANES), F32),
             pltpu.VMEM((rows, LANES), F32),
             pltpu.VMEM((rows, LANES), F32),
@@ -930,7 +957,6 @@
             pltpu.VMEM((LANES, 1), F32),
             pltpu.VMEM((8, pixels), F32),
             pltpu.VMEM((8, pixels), F32),
-            pltpu.VMEM((pixels // LANES, LANES), F32),
             dma((4 + steps,)),
             dma((steps + 1,)),
             dma((steps + 1,)),
@@ -950,10 +976,37 @@
     )(imagery, index, yields, mask)
 
 
+def finish_kernel(
+    fit_ref, spread_in, index_ref, yield_ref, fitted_ref, spread_ref, resid_ref
+):
+    rows = fit_ref.shape[0]
+    fit = fit_ref[...]
+    high, low = one_hots(index_ref[...], rows)
+    low = jnp.where(low, 1.0, 0.0).astype(BF16)
+    table = jnp.concatenate(split3(fit), 0)
+    found = jnp.dot(table, low, preferred_element_type=F32)
+    found = found[:rows] + (found[rows : 2 * rows] + found[2 * rows :])
+    value = jnp.sum(jnp.where(high, found, 0.0), 0, keepdims=True)
+    resid_ref[...] = yield_ref[...] - value
+    for r in range(rows):
+        fitted_ref[:, r * LANES : (r + 1) * LANES] = fit[r : r + 1]
+    spread_ref[...] = spread_in[...]
+
+
+def finish(fit, spread, index, yields):
+    shape = jax.ShapeDtypeStruct(spread.shape, F32)
+    return pl.pallas_call(
+        finish_kernel,
+        out_shape=(shape, shape, shape),
+        compiler_params=pltpu.CompilerParams(vmem_limit_bytes=16 * 1024 * 1024),
+        name="finish",
+    )(fit, spread, index, yields)
+
+
 def on_device_fused(imagery, pixel_mask, point_pixel, point_yield):
     pixels = imagery.shape[3]
     mask = pixel_mask.reshape(pixels // LANES, LANES)
-    fitted, spread, resid = fused(imagery, point_pixel, point_yield, mask)
+    fitted, spread, resid = finish(*fused(imagery, point_pixel, point_yield, mask))
     return (fitted[None], spread[None], resid[None])
 
 

time: 73.6 us -> 66.9 us (0.909)
  local copies, waits for them, and re-layouts: 3.97 us -> 0 us
  Pallas kernels: 68.6 us -> 66.1 us
    unnamed x3 -> x0, local copies, waits for them, and re-layouts: 3.97 us -> none
    pallas_call x1, Pallas kernels: 68.6 us -> 65.1 us  [fused(): pl.pallas_call(functools.partial(fused_kernel, lax.axis_size('tiles')), o...]
    pallas_call x0 -> x1, Pallas kernels: none -> 1.02 us  [finish(): pl.pallas_call(finish_kernel, out_shape=(shape, shape, shape), compiler_p...]
where the time goes in v3:
time: 66.9 us; the launch traced here: 66.7 us
  Pallas kernels  66.1 us (99%)
    pallas_call x1, Pallas kernels, fused(): pl.pallas_call(functools.partial(fused_kernel, lax.axis_size('tiles')), o...  65.1 us

profile of v3, /device:TPU:0, one launch (start us, length us, event | category | flops | bytes accessed | tf_op | source)
XLA Modules:
  0.0 66.7 jit_solution(4492909616922348962)
XLA Ops:
  0.6 65.1 %fused.1 = (f32[32,128]{1,0:T(8,128)S(1)}, f32[1,4096]{1,0:T(1,128)S(1)}, s32[1,4096]{1,0:T(1,128)S(1)}, f32[1,4096]{1,0:T(1,128)S(1)}) custom-call(bf16[1,2,216,4096]{3,2,1,0:T(8,128)(2,1)} %img.1, s32[1,1,4096]{2,1,0:T(1,128)} %index_hbm.1, f32[1,1,4096]{2,1,0:T(1,128)} %yield_hbm.1, s32[32,128]{1,0:T(8,128)} %bitcast.4), custom_call_target="tpu_custom_call" | custom-call | tf_op jit(solution)/shard_map/fused/pallas_call | solution.py:929
  65.7 1.0 %finish.1 = (f32[1,4096]{1,0:T(1,128)}, f32[1,4096]{1,0:T(1,128)}, f32[1,4096]{1,0:T(1,128)}) custom-call(f32[32,128]{1,0:T(8,128)S(1)} %get-tuple-element.10.fit_ref, f32[1,4096]{1,0:T(1,128)S(1)} %get-tuple-element.11.spread_in, s32[1,4096]{1,0:T(1,128)S(1)} %get-tuple-element.12.index_ref, f32[1,4096]{1,0:T(1,128)S(1)} %get-tuple-element.13.yield_ref), custom_call_target="tpu_custom_call" | custom-call | tf_op jit(solution)/shard_map/finish/pallas_call | solution.py:998

commit v4 on v3

--- a/solution.py
+++ b/solution.py
@@ -442,7 +442,7 @@
 
 
 def payload_rows(full, k):
-    return (128 if k < full else 48) * (k + 1) + 8
+    return 128 * k + 64 + 8 if k < full else 48 * k + 24 + 8
 
 
 def payload_starts(full):
@@ -451,6 +451,37 @@
         starts.append(at)
         at += payload_rows(full, k)
     return starts, at
+
+
+def pack_square(block):
+    top, bottom = block[:64], block[64:]
+    lane = lax.broadcasted_iota(jnp.int32, top.shape, 1)
+    line = lax.broadcasted_iota(jnp.int32, top.shape, 0)
+    packed = jnp.where(line >= lane - 64, bottom, pltpu.roll(top, 64, 1))
+    diagonal = jnp.sum(jnp.where(line == lane, top, 0.0), 0, keepdims=True)
+    return packed, diagonal
+
+
+def unpack_square(packed, diagonal):
+    lane = lax.broadcasted_iota(jnp.int32, packed.shape, 1)
+    line = lax.broadcasted_iota(jnp.int32, packed.shape, 0)
+    flipped = jnp.concatenate([packed, packed], 0).T
+    corner = jnp.where(line < lane, pltpu.roll(packed, 64, 1), flipped[64:])
+    corner = jnp.where(line == lane, diagonal, corner)
+    top = jnp.where(lane < 64, corner, flipped[:64])
+    bottom = jnp.where(line >= lane - 64, packed, flipped[64:])
+    return jnp.concatenate([top, bottom], 0)
+
+
+def fold(block):
+    lane = lax.broadcasted_iota(jnp.int32, (24, LANES), 1)
+    return jnp.where(lane < 64, block[:24], pltpu.roll(block[24:], 64, 1))
+
+
+def unfold(block):
+    lane = lax.broadcasted_iota(jnp.int32, (48, LANES), 1)
+    both = jnp.concatenate([block, pltpu.roll(block, 64, 1)], 0)
+    return jnp.where(lane < 64, both, 0.0)
 
 
 def squeeze(block):
@@ -771,19 +802,23 @@
 
         lax.fori_loop(0, pixels // SPAN, chunk, 0)
         at = starts[k]
+        diagonal = jnp.zeros((1, LANES), F32)
         for j in range(k + 1):
-            if k < full:
-                block = acc[128 * j : 128 * j + 128, :LANES]
-            else:
-                block = acc[128 * j : 128 * j + 128, :LANES].T
-                block = squeeze(block)
+            block = acc[128 * j : 128 * j + 128, :LANES]
+            if k == full:
+                block = squeeze(block.T)
+            if j == k and k < full:
+                block, diagonal = pack_square(block)
+            if j == k and k == full:
+                block = fold(block)
             own[at : at + block.shape[0]] = block
             at += block.shape[0]
         moment = acc[base : base + 128, count : count + 1]
         moment = moment + acc[base : base + 128, count + 1 : count + 2]
         moment = moment + acc[base : base + 128, count + 2 : count + 3]
         moment = jnp.broadcast_to(moment, (LANES, LANES)).T
-        own[at : at + 8] = moment[:8]
+        line8 = lax.broadcasted_iota(jnp.int32, (8, LANES), 0)
+        own[at : at + 8] = jnp.where(line8 == 0, moment[:8], diagonal)
         pl.when(has_up)(lambda: z_copy(0, k, up).start())
         pl.when(has_down)(lambda: z_copy(1, k, down).start())
 
@@ -824,10 +859,15 @@
         base = 128 * k
         window = (middle[at] + 0.5 * landed[3, at]) * scale
         step = 128 if k < full else 48
-        blocks = [window[j * step : (j + 1) * step] for j in range(k + 1)]
-        if k == full:
+        blocks = [window[j * step : (j + 1) * step] for j in range(k)]
+        ends = window[payload_rows(full, k) - 8 :]
+        rhs_ref[:, base : base + 128] = ends
+        square = window[k * step : payload_rows(full, k) - 8]
+        if k < full:
+            blocks.append(unpack_square(square, ends[1:2]))
+        else:
+            blocks.append(unfold(square))
             blocks = [stretch(block) for block in blocks]
-        rhs_ref[:, base : base + 128] = window[(k + 1) * step : (k + 1) * step + 8]
         lane = lax.broadcasted_iota(jnp.int32, (count, LANES), 1)
         line = lax.broadcasted_iota(jnp.int32, (count, LANES), 0)
         pivot = blocks[k] + jnp.where(lane == line, ridge_term, 0.0)

time: 66.9 us -> 66 us (0.987)
  Pallas kernels: 66.1 us -> 65.2 us
    pallas_call x1, Pallas kernels: 65.1 us -> 64.1 us  [fused(): pl.pallas_call(functools.partial(fused_kernel, lax.axis_size('tiles')), o...]
where the time goes in v4:
time: 66 us; the launch traced here: 65.8 us
  Pallas kernels  65.2 us (99%)
    pallas_call x1, Pallas kernels, fused(): pl.pallas_call(functools.partial(fused_kernel, lax.axis_size('tiles')), o...  64.1 us

profile of v4, /device:TPU:0, one launch (start us, length us, event | category | flops | bytes accessed | tf_op | source)
XLA Modules:
  0.0 65.8 jit_solution(7154740355223817056)
XLA Ops:
  0.6 64.1 %fused.1 = (f32[32,128]{1,0:T(8,128)S(1)}, f32[1,4096]{1,0:T(1,128)S(1)}, s32[1,4096]{1,0:T(1,128)S(1)}, f32[1,4096]{1,0:T(1,128)S(1)}) custom-call(bf16[1,2,216,4096]{3,2,1,0:T(8,128)(2,1)} %img.1, s32[1,1,4096]{2,1,0:T(1,128)} %index_hbm.1, f32[1,1,4096]{2,1,0:T(1,128)} %yield_hbm.1, s32[32,128]{1,0:T(8,128)} %bitcast.4), custom_call_target="tpu_custom_call" | custom-call | tf_op jit(solution)/shard_map/fused/pallas_call | solution.py:969
  64.8 1.0 %finish.1 = (f32[1,4096]{1,0:T(1,128)}, f32[1,4096]{1,0:T(1,128)}, f32[1,4096]{1,0:T(1,128)}) custom-call(f32[32,128]{1,0:T(8,128)S(1)} %get-tuple-element.10.fit_ref, f32[1,4096]{1,0:T(1,128)S(1)} %get-tuple-element.11.spread_in, s32[1,4096]{1,0:T(1,128)S(1)} %get-tuple-element.12.index_ref, f32[1,4096]{1,0:T(1,128)S(1)} %get-tuple-element.13.yield_ref), custom_call_target="tpu_custom_call" | custom-call | tf_op jit(solution)/shard_map/finish/pallas_call | solution.py:1038

commit v5 on v4

--- a/solution.py
+++ b/solution.py
@@ -540,13 +540,15 @@
     return terms[0]
 
 
-def block_factor(block, groups):
+def block_factor(block, groups, midway=None):
     rows = block.shape[0]
     lane = lax.broadcasted_iota(jnp.int32, (8, LANES), 1)
     line = lax.broadcasted_iota(jnp.int32, (8, LANES), 0)
     result = [jnp.zeros((8, LANES), F32)] * (rows // 8)
     below, first = block, 0
     for g in groups:
+        if midway is not None and g == 12:
+            midway()
         k = 8 * g
         below = below[k - first :]
         top = below[:8]
@@ -744,35 +746,39 @@
     fit8[...] = jnp.zeros_like(fit8)
     spread8[...] = jnp.zeros_like(spread8)
 
-    def payload(k):
-        return pl.ds(starts[k], payload_rows(full, k))
-
-    def z_copy(way, k, target):
+    def payload(k, h):
+        count = payload_rows(full, k)
+        first = count // 16 * 8
+        if h == 0:
+            return pl.ds(starts[k], first)
+        return pl.ds(starts[k] + first, count - first)
+
+    def z_copy(way, k, h, target):
         return pltpu.make_async_remote_copy(
-            src_ref=own.at[payload(k)],
-            dst_ref=landed.at[way, payload(k)],
-            send_sem=z_send.at[way, k],
-            recv_sem=z_recv.at[way, k],
+            src_ref=own.at[payload(k, h)],
+            dst_ref=landed.at[way, payload(k, h)],
+            send_sem=z_send.at[way, 2 * k + h],
+            recv_sem=z_recv.at[way, 2 * k + h],
             device_id=target,
             device_id_type=mesh_ids,
         )
 
-    def core_copy(k):
+    def core_copy(k, h):
         return pltpu.make_async_remote_copy(
-            src_ref=middle.at[payload(k)],
-            dst_ref=landed.at[2, payload(k)],
-            send_sem=core_send.at[k],
-            recv_sem=core_recv.at[k],
+            src_ref=middle.at[payload(k, h)],
+            dst_ref=landed.at[2, payload(k, h)],
+            send_sem=core_send.at[2 * k + h],
+            recv_sem=core_recv.at[2 * k + h],
             device_id=core,
             device_id_type=mesh_ids,
         )
 
-    def x_copy(k):
+    def x_copy(k, h, source=outgoing):
         return pltpu.make_async_remote_copy(
-            src_ref=outgoing.at[payload(k)],
-            dst_ref=landed.at[3, payload(k)],
-            send_sem=x_send.at[k],
-            recv_sem=x_recv.at[k],
+            src_ref=source.at[payload(k, h)],
+            dst_ref=landed.at[3, payload(k, h)],
+            send_sem=x_send.at[2 * k + h],
+            recv_sem=x_recv.at[2 * k + h],
             device_id=across,
             device_id_type=mesh_ids,
         )
@@ -819,42 +825,50 @@
         moment = jnp.broadcast_to(moment, (LANES, LANES)).T
         line8 = lax.broadcasted_iota(jnp.int32, (8, LANES), 0)
         own[at : at + 8] = jnp.where(line8 == 0, moment[:8], diagonal)
-        pl.when(has_up)(lambda: z_copy(0, k, up).start())
-        pl.when(has_down)(lambda: z_copy(1, k, down).start())
+        for h in range(2):
+            pl.when(has_up)(lambda h=h: z_copy(0, k, h, up).start())
+            pl.when(has_down)(lambda h=h: z_copy(1, k, h, down).start())
 
     def z_join(k):
-        at = payload(k)
-        middle[at] = own[at]
-
-        @pl.when(has_down)
-        def _():
-            z_copy(0, k, down).wait_recv()
-            middle[at] += 0.5 * landed[0, at]
-
-        @pl.when(has_up)
-        def _():
-            z_copy(1, k, up).wait_recv()
-            middle[at] += 0.5 * landed[1, at]
-
-        @pl.when(jnp.logical_not(joins))
-        def _():
-            core_copy(k).start()
-            outgoing[at] = middle[at]
+        for h in range(2):
+            at = payload(k, h)
+
+            @pl.when(has_down)
+            def _(h=h, at=at):
+                z_copy(0, k, h, down).wait_recv()
+                middle[at] = own[at] + 0.5 * landed[0, at]
+
+            @pl.when(jnp.logical_not(has_down))
+            def _(at=at):
+                middle[at] = own[at]
+
+            @pl.when(has_up)
+            def _(h=h, at=at):
+                z_copy(1, k, h, up).wait_recv()
+                middle[at] += 0.5 * landed[1, at]
+
+            @pl.when(jnp.logical_not(joins))
+            def _(h=h):
+                core_copy(k, h).start()
+                x_copy(k, h, middle).start()
 
         @pl.when(joins)
         def _():
-            core_copy(k).wait_recv()
-            outgoing[at] = middle[at] + landed[2, at]
-
-        x_copy(k).start()
+            for h in range(2):
+                at = payload(k, h)
+                core_copy(k, h).wait_recv()
+                outgoing[at] = middle[at] + landed[2, at]
+                x_copy(k, h).start()
+
         if k + 2 < steps:
             bulk[k + 2].start()
         if k + 2 == full:
             bulk[steps].start()
 
-    def solve(k):
-        at = payload(k)
-        x_copy(k).wait_recv()
+    def solve(k, midway=None):
+        at = pl.ds(starts[k], payload_rows(full, k))
+        for h in range(2):
+            x_copy(k, h).wait_recv()
         count = step_rows(full, k)
         base = 128 * k
         window = (middle[at] + 0.5 * landed[3, at]) * scale
@@ -889,7 +903,7 @@
                 )
             pivot = pivot - drop
         groups = range(16) if k < full else (0, 1, 2, 4, 5, 6)
-        lower = block_factor(pivot, groups)
+        lower = block_factor(pivot, groups, midway)
         if k:
             lower = jnp.concatenate([-dot32(lower[:, :count], coupling), lower], 1)
         z_ref[:count] = jnp.sum(
@@ -933,27 +947,26 @@
 
     gram(0)
     z_join(0)
-    for k in range(1, steps - 1):
+    for k in range(1, steps):
         gram(k)
-        solve(k - 1)
-        z_join(k)
-        if k < steps - 2:
+        if k == full:
+            spread(k - 2)
+        solve(k - 1, lambda k=k: z_join(k))
+        if k != full - 1:
             spread(k - 1)
-    gram(full)
-    spread(full - 2)
-    z_join(full)
-    solve(full - 1)
-    spread(full - 1)
     solve(full)
     spread(full)
 
     for copy in bulk:
         copy.wait_send()
     for k in range(steps):
-        pl.when(has_up)(lambda k=k: z_copy(0, k, up).wait_send())
-        pl.when(has_down)(lambda k=k: z_copy(1, k, down).wait_send())
-        pl.when(jnp.logical_not(joins))(lambda k=k: core_copy(k).wait_send())
-        x_copy(k).wait_send()
+        for h in range(2):
+            pl.when(has_up)(lambda k=k, h=h: z_copy(0, k, h, up).wait_send())
+            pl.when(has_down)(lambda k=k, h=h: z_copy(1, k, h, down).wait_send())
+            pl.when(jnp.logical_not(joins))(
+                lambda k=k, h=h: core_copy(k, h).wait_send()
+            )
+            x_copy(k, h).wait_send()
 
 
 def fused(imagery, index, yields, mask):
@@ -1000,12 +1013,12 @@
             dma((4 + steps,)),
             dma((steps + 1,)),
             dma((steps + 1,)),
-            dma((2, steps)),
-            dma((2, steps)),
-            dma((steps,)),
-            dma((steps,)),
-            dma((steps,)),
-            dma((steps,)),
+            dma((2, 2 * steps)),
+            dma((2, 2 * steps)),
+            dma((2 * steps,)),
+            dma((2 * steps,)),
+            dma((2 * steps,)),
+            dma((2 * steps,)),
         ],
         compiler_params=pltpu.CompilerParams(
             collective_id=1,

time: 66 us -> 65 us (0.985)
  Pallas kernels: 65.2 us -> 64.2 us
    pallas_call x1, Pallas kernels: 64.1 us -> 63.2 us  [fused(): pl.pallas_call(functools.partial(fused_kernel, lax.axis_size('tiles')), o...]
where the time goes in v5:
time: 65 us; the launch traced here: 64.8 us
  Pallas kernels  64.2 us (99%)
    pallas_call x1, Pallas kernels, fused(): pl.pallas_call(functools.partial(fused_kernel, lax.axis_size('tiles')), o...  63.2 us

profile of v5, /device:TPU:0, one launch (start us, length us, event | category | flops | bytes accessed | tf_op | source)
XLA Modules:
  0.0 64.8 jit_solution(7394011603547176373)
XLA Ops:
  0.6 63.2 %fused.1 = (f32[32,128]{1,0:T(8,128)S(1)}, f32[1,4096]{1,0:T(1,128)S(1)}, s32[1,4096]{1,0:T(1,128)S(1)}, f32[1,4096]{1,0:T(1,128)S(1)}) custom-call(bf16[1,2,216,4096]{3,2,1,0:T(8,128)(2,1)} %img.1, s32[1,1,4096]{2,1,0:T(1,128)} %index_hbm.1, f32[1,1,4096]{2,1,0:T(1,128)} %yield_hbm.1, s32[32,128]{1,0:T(8,128)} %bitcast.4), custom_call_target="tpu_custom_call" | custom-call | tf_op jit(solution)/shard_map/fused/pallas_call | solution.py:982
  63.8 1.0 %finish.1 = (f32[1,4096]{1,0:T(1,128)}, f32[1,4096]{1,0:T(1,128)}, f32[1,4096]{1,0:T(1,128)}) custom-call(f32[32,128]{1,0:T(8,128)S(1)} %get-tuple-element.10.fit_ref, f32[1,4096]{1,0:T(1,128)S(1)} %get-tuple-element.11.spread_in, s32[1,4096]{1,0:T(1,128)S(1)} %get-tuple-element.12.index_ref, f32[1,4096]{1,0:T(1,128)S(1)} %get-tuple-element.13.yield_ref), custom_call_target="tpu_custom_call" | custom-call | tf_op jit(solution)/shard_map/finish/pallas_call | solution.py:1051

commit v6 on v5

--- a/solution.py
+++ b/solution.py
@@ -906,12 +906,18 @@
         lower = block_factor(pivot, groups, midway)
         if k:
             lower = jnp.concatenate([-dot32(lower[:, :count], coupling), lower], 1)
-        z_ref[:count] = jnp.sum(
+        row = 128 if k == full else 0
+        low_at = (192 if k >= full - 1 else count) + row
+        z_ref[row : row + count] = jnp.sum(
             lower * rhs_ref[:1, : base + 128], 1, keepdims=True
         )
         high, low = split2(lower)
-        split_r[:count, : base + 128] = high
-        split_r[count : 2 * count, : base + 128] = low
+        split_r[row : row + count, : base + 128] = high
+        split_r[low_at : low_at + count, : base + 128] = low
+        if k == full - 1:
+            gap = jnp.zeros((count, 128), BF16)
+            split_r[:count, base + 128 :] = gap
+            split_r[low_at : low_at + count, base + 128 :] = gap
         if k < full:
             inverse[base : base + count, : base + 128] = lower
 
@@ -919,6 +925,8 @@
         count = step_rows(full, k)
         end = 128 * k + count
         last = k == full
+        if last:
+            count = 192
 
         def chunk(i, _):
             at = pl.ds(pl.multiple_of(i * SPAN, SPAN), SPAN)
@@ -952,7 +960,7 @@
         if k == full:
             spread(k - 2)
         solve(k - 1, lambda k=k: z_join(k))
-        if k != full - 1:
+        if k == 1:
             spread(k - 1)
     solve(full)
     spread(full)
@@ -1005,9 +1013,9 @@
             pltpu.VMEM((rows, LANES), F32),
             pltpu.VMEM((4, rows, LANES), F32),
             pltpu.VMEM((size, size), F32),
-            pltpu.VMEM((2 * LANES, size), BF16),
+            pltpu.VMEM((3 * LANES, size), BF16),
             pltpu.VMEM((8, size), F32),
-            pltpu.VMEM((LANES, 1), F32),
+            pltpu.VMEM((192, 1), F32),
             pltpu.VMEM((8, pixels), F32),
             pltpu.VMEM((8, pixels), F32),
             dma((4 + steps,)),

time: 65 us -> 66 us (1.015)
  Pallas kernels: 64.2 us -> 65.2 us
    pallas_call x1, Pallas kernels: 63.2 us -> 64.2 us  [fused(): pl.pallas_call(functools.partial(fused_kernel, lax.axis_size('tiles')), o...]
where the time goes in v6:
time: 66 us; the launch traced here: 65.9 us
  Pallas kernels  65.2 us (99%)
    pallas_call x1, Pallas kernels, fused(): pl.pallas_call(functools.partial(fused_kernel, lax.axis_size('tiles')), o...  64.2 us

profile of v6, /device:TPU:0, one launch (start us, length us, event | category | flops | bytes accessed | tf_op | source)
XLA Modules:
  0.0 65.9 jit_solution(7139516079797272043)
XLA Ops:
  0.6 64.2 %fused.1 = (f32[32,128]{1,0:T(8,128)S(1)}, f32[1,4096]{1,0:T(1,128)S(1)}, s32[1,4096]{1,0:T(1,128)S(1)}, f32[1,4096]{1,0:T(1,128)S(1)}) custom-call(bf16[1,2,216,4096]{3,2,1,0:T(8,128)(2,1)} %img.1, s32[1,1,4096]{2,1,0:T(1,128)} %index_hbm.1, f32[1,1,4096]{2,1,0:T(1,128)} %yield_hbm.1, s32[32,128]{1,0:T(8,128)} %bitcast.4), custom_call_target="tpu_custom_call" | custom-call | tf_op jit(solution)/shard_map/fused/pallas_call | solution.py:990
  64.9 1.0 %finish.1 = (f32[1,4096]{1,0:T(1,128)}, f32[1,4096]{1,0:T(1,128)}, f32[1,4096]{1,0:T(1,128)}) custom-call(f32[32,128]{1,0:T(8,128)S(1)} %get-tuple-element.10.fit_ref, f32[1,4096]{1,0:T(1,128)S(1)} %get-tuple-element.11.spread_in, s32[1,4096]{1,0:T(1,128)S(1)} %get-tuple-element.12.index_ref, f32[1,4096]{1,0:T(1,128)S(1)} %get-tuple-element.13.yield_ref), custom_call_target="tpu_custom_call" | custom-call | tf_op jit(solution)/shard_map/finish/pallas_call | solution.py:1059

commit v7 on v5

--- a/solution.py
+++ b/solution.py
@@ -547,7 +547,7 @@
     result = [jnp.zeros((8, LANES), F32)] * (rows // 8)
     below, first = block, 0
     for g in groups:
-        if midway is not None and g == 12:
+        if midway is not None and g == 10:
             midway()
         k = 8 * g
         below = below[k - first :]

time: 65 us -> 64.6 us (level)
  no operation moved by 1% of the time
where the time goes in v7:
time: 64.6 us; the launch traced here: 64.4 us
  Pallas kernels  63.8 us (99%)
    pallas_call x1, Pallas kernels, fused(): pl.pallas_call(functools.partial(fused_kernel, lax.axis_size('tiles')), o...  62.7 us

profile of v7, /device:TPU:0, one launch (start us, length us, event | category | flops | bytes accessed | tf_op | source)
XLA Modules:
  0.0 64.4 jit_solution(11843173534232934848)
XLA Ops:
  0.6 62.7 %fused.1 = (f32[32,128]{1,0:T(8,128)S(1)}, f32[1,4096]{1,0:T(1,128)S(1)}, s32[1,4096]{1,0:T(1,128)S(1)}, f32[1,4096]{1,0:T(1,128)S(1)}) custom-call(bf16[1,2,216,4096]{3,2,1,0:T(8,128)(2,1)} %img.1, s32[1,1,4096]{2,1,0:T(1,128)} %index_hbm.1, f32[1,1,4096]{2,1,0:T(1,128)} %yield_hbm.1, s32[32,128]{1,0:T(8,128)} %bitcast.4), custom_call_target="tpu_custom_call" | custom-call | tf_op jit(solution)/shard_map/fused/pallas_call | solution.py:982
  63.4 1.0 %finish.1 = (f32[1,4096]{1,0:T(1,128)}, f32[1,4096]{1,0:T(1,128)}, f32[1,4096]{1,0:T(1,128)}) custom-call(f32[32,128]{1,0:T(8,128)S(1)} %get-tuple-element.10.fit_ref, f32[1,4096]{1,0:T(1,128)S(1)} %get-tuple-element.11.spread_in, s32[1,4096]{1,0:T(1,128)S(1)} %get-tuple-element.12.index_ref, f32[1,4096]{1,0:T(1,128)S(1)} %get-tuple-element.13.yield_ref), custom_call_target="tpu_custom_call" | custom-call | tf_op jit(solution)/shard_map/finish/pallas_call | solution.py:1051
